TPU v7x, 128 devices: a whole 4x4x4 slice. The times are simulated.
128 devices in a mesh: theta: 16 (over z, x_hi, core), ax: 8 (over x_lo, y).
Axes of the slice: x: 4 (x_hi: 2, x_lo: 2; x = x_hi * 2 + x_lo), y: 4, z: 4, core: 2. Of those that a mesh axis runs over, the one named last changes fastest.
Arguments:
- state: float32 [5, 1024, 64, 1024], P(None, 'theta', None, 'ax'), as said below
- viscosity: float32 [1024, 64, 1024], P('theta', None, 'ax'), may hold values from 0.05 to 0.5
- band_rims: float32 [5, 1024, 4, 1024], P(None, 'theta', None, 'ax'), as said below
- coupling: float32 [5, 5], replicated, may hold values from -2.5 to 2.5
- block_map: int32 [8], replicated, may hold values from 0 to 7, as said below
- plane_flags: int32 [8], replicated, may hold values from 0 to 3
- mode_cutoff: int32 [1], replicated, may hold values from 2 to 256
Outputs:
- updated: float32 [5, 1024, 64, 1024], P(None, 'theta', None, 'ax')
Inputs may be any that keep to these rules, and one draw needn't show every extreme that they name: `block_map`: entries of plane_flags; the values 0 and 7 both appear. `state`: density within 0.8 to 1.2, momenta within -1 to 1, energy within 2 to 3. `band_rims`: density within 0.8 to 1.2, momenta within -1 to 1, energy within 2 to 3.
All inputs are finite; a program needn't handle non-finite values.
Results may differ from a plain program's by a relative error of at most 0.0003.
Values sent between devices are 32-bit elements; how exact they have to be, the bound alone decides.
A program may use at most 640 MiB of HBM per device.

v0:
```python
import functools
import math

import jax
import jax.numpy as jnp
import numpy as np
from jax import lax
from jax.experimental import pallas as pl
from jax.experimental.pallas import tpu as pltpu
from jax.sharding import PartitionSpec as P

UNIT = 0.2 / 12.0
V = 5
T = 64
R = 64
X = 128
TILE = 8
PAD = R + 2 * TILE
GROUPS = 4
PER = 16
CHUNK = 8
ROWS = 24
MESH = pl.DeviceIdType.MESH


def inverse_of(density):
    guess = pl.reciprocal(density, approx=True)
    return guess * (2.0 - density * guess)


def velocities(q):
    inv = inverse_of(q[0])
    u, v, w = q[1] * inv, q[2] * inv, q[3] * inv
    p = 0.4 * (q[4] - 0.5 * (q[1] * u + q[2] * v + q[3] * w))
    return u, v, w, p, q[4] + p


def flux_x(q, vel):
    u, v, w, p, h = vel
    return [q[1], q[1] * u + p, q[2] * u, q[3] * u, h * u]


def flux_r(q, vel):
    u, v, w, p, h = vel
    return [q[2], q[2] * u, q[2] * v + p, q[3] * v, h * v]


def flux_t(q, vel):
    u, v, w, p, h = vel
    return [q[3], q[3] * u, q[3] * v, q[3] * w + p, h * w]


def roll(x, shift):
    return pltpu.roll(x, shift % X, 1)


def lanes_of(rows=TILE):
    return lax.broadcasted_iota(jnp.int32, (rows, X), 1)


def section_body(
    state, visc, rims, sector, edges, out,
    q, nu, rim, edg, fr, ft, res, in_sem, misc_sem, out_sem,
):
    n_chunks = T // CHUNK

    def fetch(c):
        t0 = c * CHUNK
        return (
            pltpu.make_async_copy(
                state.at[:, pl.ds(t0, CHUNK)],
                q.at[:, pl.ds(t0 + 2, CHUNK), pl.ds(TILE, R)],
                in_sem.at[0, c],
            ),
            pltpu.make_async_copy(
                visc.at[pl.ds(t0, CHUNK)], nu.at[pl.ds(t0, CHUNK)], in_sem.at[1, c]
            ),
        )

    misc = [
        pltpu.make_async_copy(sector.at[0], q.at[:, pl.ds(0, 2), pl.ds(TILE, R)], misc_sem.at[0]),
        pltpu.make_async_copy(
            sector.at[1], q.at[:, pl.ds(T + 2, 2), pl.ds(TILE, R)], misc_sem.at[1]
        ),
        pltpu.make_async_copy(rims, rim, misc_sem.at[2]),
        pltpu.make_async_copy(edges, edg, misc_sem.at[3]),
    ]
    misc[0].start()
    for copy in fetch(0):
        copy.start()
    for copy in misc[1:]:
        copy.start()
    for c in range(1, n_chunks):
        for copy in fetch(c):
            copy.start()

    lane = lanes_of()
    edge_lanes = (lane < 2) | (lane >= X - 2)

    def circum_only(s):
        for k in range(R // TILE):
            rows = pl.ds(TILE + k * TILE, TILE)
            cell = [q[v, s, rows, :] for v in range(V)]
            f = flux_t(cell, velocities(cell))
            for v in range(1, V):
                ft[v - 1, s, pl.ds(k * TILE, TILE), :] = f[v]

    def first_half(s):
        t = s - 2
        for v in range(V):
            q[v, s, pl.ds(TILE - 2, 2), :] = rim[v, t, pl.ds(0, 2), :]
            q[v, s, pl.ds(TILE + R, 2), :] = rim[v, t, pl.ds(2, 2), :]
        cell = [rim[v, t, :, :] for v in range(V)]
        f = flux_r(cell, velocities(cell))
        for v in range(1, V):
            fr[v - 1, t, pl.ds(TILE - 2, 2), :] = f[v][0:2]
            fr[v - 1, t, pl.ds(TILE + R, 2), :] = f[v][2:4]
        for k in range(R // TILE):
            rows = pl.ds(k * TILE, TILE)
            wide = pl.ds(TILE + k * TILE, TILE)
            cell = [q[v, s, wide, :] for v in range(V)]
            vel = velocities(cell)
            f = flux_r(cell, vel)
            for v in range(1, V):
                fr[v - 1, t, wide, :] = f[v]
            f = flux_t(cell, vel)
            for v in range(1, V):
                ft[v - 1, s, rows, :] = f[v]
            f = flux_x(cell, vel)
            n = nu[t, rows, :]
            n12 = 12.0 * n
            kq = 60.0 - 72.0 * n
            for v in range(V):
                near = roll(f[v], -1) - roll(f[v], 1)
                far = roll(f[v], -2) - roll(f[v], 2)
                side = roll(cell[v], -1) + roll(cell[v], 1)
                res[v, t, rows, :] = kq * cell[v] + n12 * side - 8.0 * near + far

    def second_half(t):
        s = t + 2
        group = t // PER
        back = X - 4 + (-8 * (t % PER))
        back = lax.rem(back + X, X)
        for k in range(R // TILE):
            rows = pl.ds(k * TILE, TILE)
            base = TILE + k * TILE
            n12 = 12.0 * nu[t, rows, :]
            for v in range(V):

                def rad(o):
                    at = pl.ds(base + o, TILE)
                    return q[2, s, at, :] if v == 0 else fr[v - 1, t, at, :]

                def cir(o):
                    if v == 0:
                        return q[3, s + o, pl.ds(base, TILE), :]
                    return ft[v - 1, s + o, rows, :]

                near = (rad(1) - rad(-1)) + (cir(1) - cir(-1))
                far = (rad(2) - rad(-2)) + (cir(2) - cir(-2))
                side = (q[v, s, pl.ds(base + 1, TILE), :] + q[v, s, pl.ds(base - 1, TILE), :]) + (
                    q[v, s + 1, pl.ds(base, TILE), :] + q[v, s - 1, pl.ds(base, TILE), :]
                )
                got = UNIT * (res[v, t, rows, :] + n12 * side - 8.0 * near + far)
                edge = pltpu.roll(edg[group, v, rows, :], back, 1)
                res[v, t, rows, :] = jnp.where(edge_lanes, edge, got)

    def send(t0, count, c):
        return pltpu.make_async_copy(
            res.at[:, pl.ds(t0, count)], out.at[:, pl.ds(t0, count)], out_sem.at[c]
        )

    misc[0].wait()
    circum_only(0)
    circum_only(1)
    for copy in fetch(0):
        copy.wait()
    misc[2].wait()
    misc[3].wait()
    first_half(2)
    first_half(3)

    def steps(low, high):
        def step(s, carry):
            first_half(s)
            second_half(s - 4)
            return carry

        lax.fori_loop(low, high, step, 0)

    steps(4, CHUNK + 2)
    send(0, CHUNK - 2, 0).start()

    def chunk(c, carry):
        for copy in fetch(c):
            copy.wait()
        steps(c * CHUNK + 2, c * CHUNK + CHUNK + 2)
        send(c * CHUNK - 2, CHUNK, c).start()
        return carry

    lax.fori_loop(1, n_chunks, chunk, 0)
    misc[1].wait()
    circum_only(T + 2)
    circum_only(T + 3)
    second_half(T - 2)
    second_half(T - 1)
    send(T - 2, 2, n_chunks).start()
    send(0, CHUNK - 2, 0).wait()

    def drain(c, carry):
        send(c * CHUNK - 2, CHUNK, c).wait()
        return carry

    lax.fori_loop(1, n_chunks, drain, 0)
    send(T - 2, 2, n_chunks).wait()


def section_call(state, visc, rims, sector, edges):
    any_space = pl.BlockSpec(memory_space=pl.ANY)
    f32 = jnp.float32
    return pl.pallas_call(
        section_body,
        out_shape=jax.ShapeDtypeStruct((V, T, R, X), f32),
        in_specs=[any_space] * 5,
        out_specs=any_space,
        scratch_shapes=[
            pltpu.VMEM((V, T + 4, PAD, X), f32),
            pltpu.VMEM((T, R, X), f32),
            pltpu.VMEM((V, T, 4, X), f32),
            pltpu.VMEM((GROUPS, V, R, X), f32),
            pltpu.VMEM((V - 1, T, PAD, X), f32),
            pltpu.VMEM((V - 1, T + 4, R, X), f32),
            pltpu.VMEM((V, T, R, X), f32),
            pltpu.SemaphoreType.DMA((2, T // CHUNK)),
            pltpu.SemaphoreType.DMA((4,)),
            pltpu.SemaphoreType.DMA((T // CHUNK + 1,)),
        ],
        compiler_params=pltpu.CompilerParams(vmem_limit_bytes=62 * 1024 * 1024),
        cost_estimate=pl.CostEstimate(
            flops=150 * V * T * R * X // 5, bytes_accessed=24_000_000, transcendentals=T * R * X
        ),
    )(state, visc, rims, sector, edges)


def spread_table(columns):
    table = np.zeros((GROUPS * X, len(columns) * X), np.float32)
    for place, j in enumerate(columns):
        for t in range(T):
            group, slot = divmod(t, PER)
            for side in range(2):
                e = 4 + j if side == 0 else 3 - j
                table[group * X + slot * 8 + e, place * X + side * T + t] = 1
    return table


def halo_table():
    table = np.zeros((X, 4 * X), np.float32)
    for j in range(2):
        for side in range(2):
            e = 4 + j if side == 0 else 3 - j
            for slot, lane in ((1, 0), (2, T - 1)):
                table[slot * 8 + e, 2 * j * X + side * T + lane] = 1
            for slot, lane in ((0, 0), (1, 1), (2, T - 2), (3, T - 1)):
                table[slot * 8 + e, (2 * j + 1) * X + side * T + lane] = 1
    return table


def split(x):
    high = x.astype(jnp.bfloat16)
    return high, (x - high.astype(jnp.float32)).astype(jnp.bfloat16)


def dot(a, b):
    return jnp.dot(a, b, preferred_element_type=jnp.float32)


def exact_dot(x, table):
    high, low = split(x)
    return dot(high, table) + dot(low, table)


def sine(n):
    rest = n & 1023
    folded = jnp.minimum(rest, 1024 - rest).astype(jnp.float32) * (math.pi / 1024)
    s = folded * folded
    p = jnp.float32(-2.5052108e-08)
    for c in (2.7557319e-06, -1.9841270e-04, 8.3333333e-03, -1.6666667e-01, 1.0):
        p = p * s + c
    p = p * folded
    return jnp.where(n < 1024, p, -p)


def edges_body(
    n_theta, n_ax,
    state, visc, rims, spread, place, halo, coupling, block_map, plane_flags, cutoff,
    edges, sector,
    q, nu, rim, tabs, tabp, tabh, hal, packed, packed_hal, edge, around, ax_out, ax_in,
    rad, sect, send_a, recv_a, send_b, recv_b, gh, gl, lhs, filt, res,
    in_sem, misc_sem, halo_send, halo_recv, ax_send, ax_recv, a_send, a_recv, b_send, b_recv, out_sem,
):
    me = lax.axis_index("theta")
    my_ax = lax.axis_index("ax")
    nxt, prv = lax.rem(me + 1, n_theta), lax.rem(me + n_theta - 1, n_theta)
    right, left = lax.rem(my_ax + 1, n_ax), lax.rem(my_ax + n_ax - 1, n_ax)
    rs = R // n_theta

    def fetch(g):
        return pltpu.make_async_copy(
            state.at[:, pl.ds(g * PER, PER)], q.at[:, pl.ds(g * PER, PER)], in_sem.at[g]
        )

    misc = [
        pltpu.make_async_copy(rims, rim, misc_sem.at[0]),
        pltpu.make_async_copy(visc, nu, misc_sem.at[1]),
        pltpu.make_async_copy(spread, tabs, misc_sem.at[2]),
        pltpu.make_async_copy(place, tabp, misc_sem.at[3]),
        pltpu.make_async_copy(halo, tabh, misc_sem.at[4]),
    ]
    for g in range(GROUPS):
        fetch(g).start()
    for copy in misc:
        copy.start()

    barrier = pltpu.get_barrier_semaphore()

    def greet(i, carry):
        pl.semaphore_signal(
            barrier, inc=1, device_id=(lax.rem(me + i, n_theta), my_ax), device_id_type=MESH
        )
        return carry

    lax.fori_loop(1, n_theta, greet, 0)
    for other in (left, right):
        pl.semaphore_signal(barrier, inc=1, device_id=(me, other), device_id_type=MESH)
    pl.semaphore_wait(barrier, n_theta + 1)

    def to_sector(i, cells, peer):
        return pltpu.make_async_remote_copy(
            src_ref=state.at[:, cells],
            dst_ref=hal.at[i],
            send_sem=halo_send.at[i],
            recv_sem=halo_recv.at[i],
            device_id=(peer, my_ax),
            device_id_type=MESH,
        )

    halos = [to_sector(0, pl.ds(T - 2, 2), nxt), to_sector(1, pl.ds(0, 2), prv)]
    for copy in halos:
        copy.start()

    lane = lanes_of()
    slot_of = lane // 8

    def pack(load, slots):
        acc = None
        for slot in range(slots):
            turned = pltpu.roll(load(slot), (8 * slot + 4) % X, 1)
            if acc is None:
                acc = turned
            else:
                acc = jnp.where(slot_of[: turned.shape[0]] == slot, turned, acc)
        return acc

    for v in range(V + 1):
        packed[v, pl.ds(R, TILE), :] = jnp.zeros((TILE, GROUPS * X), jnp.float32)
    misc[0].wait()
    misc[1].wait()
    for g in range(GROUPS):
        cols = pl.ds(g * X, X)
        for v in range(V):
            packed[v, pl.ds(R, 4), cols] = pack(lambda t: rim[v, g * PER + t], PER)
    for g in range(GROUPS):
        fetch(g).wait()
        cols = pl.ds(g * X, X)

        def rows_of(k, carry):
            rows = pl.ds(pl.multiple_of(k * TILE, TILE), TILE)
            for v in range(V):
                packed[v, rows, cols] = pack(lambda t: q[v, g * PER + t, rows, :], PER)
            packed[V, rows, cols] = pack(lambda t: nu[g * PER + t, rows, :], PER)
            return carry

        lax.fori_loop(0, R // TILE, rows_of, 0)
    for copy in misc[2:]:
        copy.wait()

    def unpack(v, carry):
        got = exact_dot(packed[v, pl.ds(0, R + TILE), :], tabs[...])
        for j in range(4):
            edge[j, v] = got[:, j * X : (j + 1) * X]
        return carry

    lax.fori_loop(0, V + 1, unpack, 0)

    first = lane < T

    def stage(k, carry):
        rows = pl.ds(pl.multiple_of(k * TILE, TILE), TILE)
        for v in range(V):
            near, far = edge[0, v, rows, :], edge[1, v, rows, :]
            ax_out[0, v, rows, :] = jnp.where(first, near, roll(far, T))
            ax_out[1, v, rows, :] = jnp.where(first, roll(near, T), far)
        return carry

    lax.fori_loop(0, R // TILE, stage, 0)

    def to_ax(i, peer):
        return pltpu.make_async_remote_copy(
            src_ref=ax_out.at[i],
            dst_ref=ax_in.at[i],
            send_sem=ax_send.at[i],
            recv_sem=ax_recv.at[i],
            device_id=(me, peer),
            device_id_type=MESH,
        )

    sides = [to_ax(0, left), to_ax(1, right)]
    for copy in sides:
        copy.start()

    twice = 2 * cutoff[0] - 1

    def weights(b, carry):
        def some(i, carry):
            rows = pl.ds(pl.multiple_of(i * 16, 16), 16)
            down = lax.broadcasted_iota(jnp.int32, (16, 256), 0) + i * 16
            along = lax.broadcasted_iota(jnp.int32, (16, 256), 1)
            tau = (b * 256 + along - down) & 1023
            top = sine((twice * tau) & 2047)
            below = sine(jnp.maximum(tau, 1))
            ratio = jnp.where(tau == 0, twice.astype(jnp.float32), top / below)
            g = (ratio - 1.0) * (1.0 / 1024)
            high, low = split(g)
            gh[b, rows, :] = high
            gl[b, rows, :] = low
            return carry

        return lax.fori_loop(0, 16, some, carry)

    lax.fori_loop(0, 4, weights, 0)

    for copy in halos:
        copy.wait_recv()

    def pack_halo(k, carry):
        rows = pl.ds(pl.multiple_of(k * TILE, TILE), TILE)
        for v in range(V):
            packed_hal[v, rows, :] = pack(lambda t: hal[t // 2, v, t % 2, rows, :], 4)
        return carry

    lax.fori_loop(0, R // TILE, pack_halo, 0)

    def unpack_halo(v, carry):
        got = exact_dot(packed_hal[v], tabh[...])
        for i in range(4):
            around[i, v] = got[:, i * X : (i + 1) * X]
        return carry

    lax.fori_loop(0, V, unpack_halo, 0)

    to_hbm = [pltpu.make_async_copy(hal, sector, out_sem.at[0])]
    to_hbm[0].start()

    def radial(k, carry):
        rows = pl.ds(pl.multiple_of(k * TILE, TILE), TILE)
        wide = pl.ds(pl.multiple_of(k * TILE + TILE, TILE), TILE)
        for j in range(2):
            cell = [edge[j, v, rows, :] for v in range(V)]
            f = flux_r(cell, velocities(cell))
            for v in range(V):
                rad[j, v, wide, :] = f[v]
                rad[j, V + v, wide, :] = cell[v]
        return carry

    lax.fori_loop(0, R // TILE, radial, 0)
    for j in range(2):
        cell = [edge[j, v, pl.ds(R, TILE), :] for v in range(V)]
        f = flux_r(cell, velocities(cell))
        for v in range(V):
            for i, kept in ((v, f[v]), (V + v, cell[v])):
                rad[j, i, pl.ds(TILE - 2, 2), :] = kept[0:2]
                rad[j, i, pl.ds(TILE + R, 2), :] = kept[2:4]

    for copy in sides:
        copy.wait_recv()

    sign = jnp.where(first, 1.0, -1.0).astype(jnp.float32)
    has_left = (my_ax > 0).astype(jnp.int32)
    has_right = (my_ax < n_ax - 1).astype(jnp.int32)
    inside = jnp.where(first, has_left, has_right) == 1
    at = lane & (T - 1)

    def section(k, carry):
        rows = pl.ds(pl.multiple_of(k * TILE, TILE), TILE)
        low = pl.multiple_of(k * TILE, TILE)
        cells, fluxes = {}, {}
        for j in range(-2, 4):
            if j >= 0:
                cell = [edge[j, v, rows, :] for v in range(V)]
            else:
                cell = []
                for v in range(V):
                    a, b = ax_in[1, v, rows, :], ax_in[0, v, rows, :]
                    if j == -1:
                        cell.append(jnp.where(first, a, roll(b, T)))
                    else:
                        cell.append(jnp.where(first, roll(a, T), b))
            vel = velocities(cell)
            f = flux_x(cell, vel)
            if j < 0:
                f = [jnp.where(inside, x, 0.0) for x in f]
                cell = [jnp.where(inside, x, 0.0) for x in cell]
            cells[j], fluxes[j] = cell, f
        for j in range(2):
            cell = cells[j]
            f = flux_t(cell, velocities(cell))
            halo_cell = [[around[2 * j + i, v, rows, :] for v in range(V)] for i in range(2)]
            halo_flux = [flux_t(c, velocities(c)) for c in halo_cell]
            n = edge[j, V, rows, :]
            n12 = 12.0 * n
            kq = 60.0 - 72.0 * n
            for v in range(V):

                def step(o, own, near, far):
                    ends = (at >= T - o) if o > 0 else (at < -o)
                    return jnp.where(ends, near if abs(o) == 1 else far, roll(own, -o))

                def cir(o):
                    return step(o, f[v], halo_flux[0][v], halo_flux[1][v])

                def cir_cell(o):
                    return step(o, cell[v], halo_cell[0][v], halo_cell[1][v])

                def r_at(i, o):
                    return rad[j, i, pl.ds(low + TILE + o, TILE), :]

                axial = 8.0 * (fluxes[j + 1][v] - fluxes[j - 1][v]) - (
                    fluxes[j + 2][v] - fluxes[j - 2][v]
                )
                near = (r_at(v, 1) - r_at(v, -1)) + (cir(1) - cir(-1))
                far = (r_at(v, 2) - r_at(v, -2)) + (cir(2) - cir(-2))
                side = (
                    (cells[j + 1][v] + cells[j - 1][v])
                    + (r_at(V + v, 1) + r_at(V + v, -1))
                    + (cir_cell(1) + cir_cell(-1))
                )
                sect[j, v, rows, :] = UNIT * (
                    kq * cell[v] + n12 * side - sign * axial - 8.0 * near + far
                )
        return carry

    lax.fori_loop(0, R // TILE, section, 0)

    for d in range(n_theta):
        send_a[d, pl.ds(V * rs, ROWS - V * rs), :] = jnp.zeros((ROWS - V * rs, X), jnp.float32)
        for v in range(V):
            send_a[d, pl.ds(v * rs, rs), :] = sect[0, v, pl.ds(d * rs, rs), :]

    def block_copy(src, dst, sems, i):
        peer = lax.rem(me + i, n_theta)
        return pltpu.make_async_remote_copy(
            src_ref=src.at[peer],
            dst_ref=dst.at[me],
            send_sem=sems[0].at[i],
            recv_sem=sems[1].at[i],
            device_id=(peer, my_ax),
            device_id_type=MESH,
        )

    def start_all(src, dst, sems):
        def go(i, carry):
            block_copy(src, dst, sems, i).start()
            return carry

        lax.fori_loop(1, n_theta, go, 0)

    def finish_all(src, dst, sems):
        def go(i, carry):
            block_copy(src, dst, sems, i).wait()
            return carry

        lax.fori_loop(1, n_theta, go, 0)

    start_all(send_a, recv_a, (a_send, a_recv))
    recv_a[me] = send_a[me]
    finish_all(send_a, recv_a, (a_send, a_recv))

    wide_first = lanes_of(ROWS) < T
    for s in range(n_theta // 2):
        a, b = recv_a[2 * s], recv_a[2 * s + 1]
        cols = pl.ds(s * X, X)
        both = [jnp.where(wide_first, a, roll(b, T)), jnp.where(wide_first, roll(a, T), b)]
        for i in range(2):
            lhs[pl.ds(i * ROWS, ROWS), cols] = both[i]

    blocks = n_theta * T // 256
    for b in range(blocks):
        total = jnp.zeros((2 * ROWS, 256), jnp.float32)
        for a in range(blocks):
            high, low = split(lhs[:, a * 256 : (a + 1) * 256])
            k = (b - a) % blocks
            total += dot(high, gh[k]) + (dot(low, gh[k]) + dot(high, gl[k]))
        filt[:, b * 256 : (b + 1) * 256] = total

    for s in range(n_theta // 2):
        cols = pl.ds(s * X, X)
        a, b = filt[pl.ds(0, ROWS), cols], filt[pl.ds(ROWS, ROWS), cols]
        send_b[2 * s] = jnp.where(wide_first, a, roll(b, T))
        send_b[2 * s + 1] = jnp.where(wide_first, roll(a, T), b)

    start_all(send_b, recv_b, (b_send, b_recv))
    recv_b[me] = send_b[me]
    finish_all(send_b, recv_b, (b_send, b_recv))

    flag = plane_flags[block_map[my_ax]]
    on = jnp.where(lanes_of(rs) < T, lax.rem(flag, 2), lax.div(flag, 2)) == 1
    for d in range(n_theta):
        mode = [recv_b[d, pl.ds(v * rs, rs), :] for v in range(V)]
        for u in range(V):
            added = coupling[u, 0] * mode[0]
            for v in range(1, V):
                added += coupling[u, v] * mode[v]
            rows = pl.ds(d * rs, rs)
            own = sect[0, u, rows, :]
            sect[0, u, rows, :] = jnp.where(on, own + added, own)

    for v in range(V):
        both = jnp.concatenate([sect[0, v], sect[1, v]], axis=1)
        got = exact_dot(both, tabp[...])
        for g in range(GROUPS):
            res[g, v] = got[:, g * X : (g + 1) * X]
    to_hbm.append(pltpu.make_async_copy(res, edges, out_sem.at[1]))
    to_hbm[1].start()
    for copy in halos + sides:
        copy.wait_send()
    for copy in to_hbm:
        copy.wait()


def edges_call(mesh, state, visc, rims, coupling, block_map, plane_flags, cutoff):
    n_theta, n_ax = mesh.shape["theta"], mesh.shape["ax"]
    any_space = pl.BlockSpec(memory_space=pl.ANY)
    smem = pl.BlockSpec(memory_space=pltpu.SMEM)
    f32, bf16 = jnp.float32, jnp.bfloat16
    tabs = spread_table(range(4))
    tables = [jnp.asarray(x, bf16) for x in (tabs, tabs[:, : 2 * X].T, halo_table())]
    dma = pltpu.SemaphoreType.DMA
    return pl.pallas_call(
        functools.partial(edges_body, n_theta, n_ax),
        out_shape=(
            jax.ShapeDtypeStruct((GROUPS, V, R, X), f32),
            jax.ShapeDtypeStruct((2, V, 2, R, X), f32),
        ),
        in_specs=[any_space] * 6 + [smem] * 4,
        out_specs=(any_space, any_space),
        scratch_shapes=[
            pltpu.VMEM((V, T, R, X), f32),
            pltpu.VMEM((T, R, X), f32),
            pltpu.VMEM((V, T, 4, X), f32),
            pltpu.VMEM((GROUPS * X, 4 * X), bf16),
            pltpu.VMEM((2 * X, GROUPS * X), bf16),
            pltpu.VMEM((X, 4 * X), bf16),
            pltpu.VMEM((2, V, 2, R, X), f32),
            pltpu.VMEM((V + 1, R + TILE, GROUPS * X), f32),
            pltpu.VMEM((V, R, X), f32),
            pltpu.VMEM((4, V + 1, R + TILE, X), f32),
            pltpu.VMEM((4, V, R, X), f32),
            pltpu.VMEM((2, V, R, X), f32),
            pltpu.VMEM((2, V, R, X), f32),
            pltpu.VMEM((2, 2 * V, PAD, X), f32),
            pltpu.VMEM((2, V, R, X), f32),
            pltpu.VMEM((n_theta, ROWS, X), f32),
            pltpu.VMEM((n_theta, ROWS, X), f32),
            pltpu.VMEM((n_theta, ROWS, X), f32),
            pltpu.VMEM((n_theta, ROWS, X), f32),
            pltpu.VMEM((4, 256, 256), bf16),
            pltpu.VMEM((4, 256, 256), bf16),
            pltpu.VMEM((2 * ROWS, n_theta * T), f32),
            pltpu.VMEM((2 * ROWS, n_theta * T), f32),
            pltpu.VMEM((GROUPS, V, R, X), f32),
            dma((GROUPS,)),
            dma((5,)),
            dma((2,)),
            dma((2,)),
            dma((2,)),
            dma((2,)),
            dma((n_theta,)),
            dma((n_theta,)),
            dma((n_theta,)),
            dma((n_theta,)),
            dma((2,)),
        ],
        compiler_params=pltpu.CompilerParams(
            collective_id=0, has_side_effects=True, vmem_limit_bytes=56 * 1024 * 1024
        ),
        cost_estimate=pl.CostEstimate(
            flops=400_000_000, bytes_accessed=14_000_000, transcendentals=0
        ),
    )(state, visc, rims, *tables, coupling, block_map, plane_flags, cutoff)


def solution(mesh):
    def local(state, viscosity, band_rims, coupling, block_map, plane_flags, mode_cutoff):
        edges, sector = edges_call(
            mesh, state, viscosity, band_rims, coupling, block_map, plane_flags, mode_cutoff
        )
        return section_call(state, viscosity, band_rims, sector, edges)

    in_specs = (
        P(None, "theta", None, "ax"),
        P("theta", None, "ax"),
        P(None, "theta", None, "ax"),
        P(),
        P(),
        P(),
        P(),
    )
    out_specs = P(None, "theta", None, "ax")
    return jax.shard_map(local, mesh=mesh, in_specs=in_specs, out_specs=out_specs, check_vma=False)
```

profile of v0, /device:TPU:1, one launch (start us, length us, event | category | flops | bytes accessed | tf_op | source)
XLA Modules:
  0.0 69.9 jit_solution(4814758194509670787)
XLA Ops:
  0.7 39.5 %shard_map.100 = (f32[4,5,64,128]{3,2,1,0:T(8,128)}, f32[2,5,2,64,128]{4,3,2,1,0:T(8,128)}) custom-call(f32[5,64,64,128]{3,2,1,0:T(8,128)} %state.3, f32[64,64,128]{2,1,0:T(8,128)} %visc.3, f32[5,64,4,128]{3,2,1,0:T(4,128)} %rims.3, bf16[512,512]{1,0:T(8,128)(2,1)} %constant.6.clone.spread, bf16[256,512]{1,0:T(8,128)(2,1)} %constant.7.clone.place, ...), custom_call_target="tpu_custom_call" | custom-call | flops 400000000 | bytes 14000000 | tf_op jit(solution)/shard_map/pallas_call | solution.py:648
  40.1 29.8 %shard_map.101 = f32[5,64,64,128]{3,2,1,0:T(8,128)} custom-call(f32[5,64,64,128]{3,2,1,0:T(8,128)} %state.3, f32[64,64,128]{2,1,0:T(8,128)} %visc.3, f32[5,64,4,128]{3,2,1,0:T(4,128)} %rims.3, f32[2,5,2,64,128]{4,3,2,1,0:T(8,128)} %get-tuple-element.7.sector, f32[4,5,64,128]{3,2,1,0:T(8,128)} %get-tuple-element.8.edges), custom_call_target="tpu_custom_call" | custom-call | flops 78643200 | bytes 24000000 | tf_op jit(solution)/shard_map/pallas_call | solution.py:221
where the time goes:
time: 70 us; the launch traced here: 69.9 us
  Pallas kernels  69.2 us (99%)
    pallas_call x1, Pallas kernels, edges_call(): pl.pallas_call(functools.partial(edges_body, n_theta, n_ax), out_shape=(j...  39.5 us
    pallas_call x1, Pallas kernels, section_call(): pl.pallas_call(section_body, out_shape=jax.ShapeDtypeStruct((V, T, R, X),...  29.8 us

commit v1 on v0

v1 whole, which is shorter than its diff:
```python
import functools
import math

import jax
import jax.numpy as jnp
import numpy as np
from jax import lax
from jax.experimental import pallas as pl
from jax.experimental.pallas import tpu as pltpu
from jax.sharding import PartitionSpec as P

UNIT = 0.2 / 12.0
V = 5
T = 64
R = 64
X = 128
TILE = 8
PAD = R + 2 * TILE
GROUPS = 4
PER = 16
CHUNK = 8
SHARE = 32
LAG = 3
ROWS = 24
MESH = pl.DeviceIdType.MESH


def inverse_of(density):
    guess = pl.reciprocal(density, approx=True)
    return guess * (2.0 - density * guess)


def velocities(q):
    inv = inverse_of(q[0])
    u, v, w = q[1] * inv, q[2] * inv, q[3] * inv
    p = 0.4 * (q[4] - 0.5 * (q[1] * u + q[2] * v + q[3] * w))
    return u, v, w, p, q[4] + p


def flux_x(q, vel):
    u, v, w, p, h = vel
    return [q[1], q[1] * u + p, q[2] * u, q[3] * u, h * u]


def flux_r(q, vel):
    u, v, w, p, h = vel
    return [q[2], q[2] * u, q[2] * v + p, q[3] * v, h * v]


def flux_t(q, vel):
    u, v, w, p, h = vel
    return [q[3], q[3] * u, q[3] * v, q[3] * w + p, h * w]


def roll(x, shift):
    return pltpu.roll(x, shift % X, 1)


def split(x):
    high = x.astype(jnp.bfloat16)
    return high, (x - high.astype(jnp.float32)).astype(jnp.bfloat16)


def dot(a, b):
    return jnp.dot(a, b, preferred_element_type=jnp.float32)


def stencil_table():
    table = np.zeros((X, X), np.float32)
    for x in range(X):
        for o, c in ((1, -8), (-1, 8), (2, 1), (-2, -1)):
            table[(x + o) % X, x] = c
    return np.concatenate([table, table])


def lanes_of(rows=TILE):
    return lax.broadcasted_iota(jnp.int32, (rows, X), 1)


def plane_maker(q, nu, rim, fr, ft, axial, res, stencil, turn_of=None, insert=None):
    pair = 2 * TILE

    def plane(s, first=True, second=True, circum=False, axial_before=True):
        q_near = q.at[:, pl.ds(s - LAG - 2, LAG + 3)] if second else q.at[:, pl.ds(s, 1)]
        ft_near = ft.at[:, pl.ds(s - LAG - 2, LAG + 3)] if second else ft.at[:, pl.ds(s, 1)]
        own = LAG + 2 if second else 0
        t = s - 2
        if second and first:
            fr_near, res_near, nu_near = (
                fr.at[:, pl.ds(t - LAG, LAG + 1)],
                res.at[:, pl.ds(t - LAG, LAG + 1)],
                nu.at[pl.ds(t - LAG, LAG + 1)],
            )
            new = LAG
        else:
            at = t - LAG if second else t
            if first or second:
                fr_near, res_near, nu_near = (
                    fr.at[:, pl.ds(at, 1)],
                    res.at[:, pl.ds(at, 1)],
                    nu.at[pl.ds(at, 1)],
                )
            new = 0

        def rims_of():
            for v in range(V):
                q_near[v, own, pl.ds(TILE - 2, 2), :] = rim[v, t, pl.ds(0, 2), :]
                q_near[v, own, pl.ds(TILE + R, 2), :] = rim[v, t, pl.ds(2, 2), :]
            cell = [rim[v, t, :, :] for v in range(V)]
            f = flux_r(cell, velocities(cell))
            for v in range(1, V):
                fr_near[v - 1, new, pl.ds(TILE - 2, 2), :] = f[v][0:2]
                fr_near[v - 1, new, pl.ds(TILE + R, 2), :] = f[v][2:4]

        def first_part(k):
            rows = pl.ds(k * pair, pair)
            wide = pl.ds(TILE + k * pair, pair)
            cell = [q_near[v, own, wide, :] for v in range(V)]
            vel = velocities(cell)
            f = flux_t(cell, vel)
            for v in range(1, V):
                ft_near[v - 1, own, rows, :] = f[v]
            if not first:
                return
            f = flux_x(cell, vel)
            for v in range(V):
                high, low = split(f[v])
                axial[v, rows, pl.ds(0, X)] = high
                axial[v, rows, pl.ds(X, X)] = low
            f = flux_r(cell, vel)
            for v in range(1, V):
                fr_near[v - 1, new, wide, :] = f[v]
            n = nu_near[new, rows, :]
            n12 = 12.0 * n
            kq = 60.0 - 72.0 * n
            for v in range(V):
                side = roll(cell[v], -1) + roll(cell[v], 1)
                res_near[v, new, rows, :] = kq * cell[v] + n12 * side

        if second:
            turn = turn_of(t - LAG) if insert is not None else None

        def second_part(k, v):
            rows = pl.ds(k * TILE, TILE)
            base = TILE + k * TILE
            n12 = 12.0 * nu_near[0, rows, :]

            def rad(o):
                at = pl.ds(base + o, TILE)
                return q_near[2, 2, at, :] if v == 0 else fr_near[v - 1, 0, at, :]

            def cir(o):
                if v == 0:
                    return q_near[3, 2 + o, pl.ds(base, TILE), :]
                return ft_near[v - 1, 2 + o, rows, :]

            near = (rad(1) - rad(-1)) + (cir(1) - cir(-1))
            far = (rad(2) - rad(-2)) + (cir(2) - cir(-2))
            side = (
                q_near[v, 2, pl.ds(base + 1, TILE), :] + q_near[v, 2, pl.ds(base - 1, TILE), :]
            ) + (q_near[v, 3, pl.ds(base, TILE), :] + q_near[v, 1, pl.ds(base, TILE), :])
            got = UNIT * (res_near[v, 0, rows, :] + n12 * side - 8.0 * near + far)
            if insert is not None:
                got = insert(turn, v, rows, got)
            res_near[v, 0, rows, :] = got

        if axial_before:
            before = res.at[:, pl.ds(t - 1, 1)] if new == 0 else res_near.at[:, pl.ds(new - 1, 1)]
            if second and not first:
                before = res.at[:, pl.ds(t - 1, 1)]
            for v in range(V):
                along = dot(axial[v], stencil[...])
                for k in range(R // pair):
                    rows = pl.ds(k * pair, pair)
                    before[v, 0, rows, :] += along[k * pair : (k + 1) * pair]
        if first:
            rims_of()
        for k in range(R // pair):
            if first or circum:
                first_part(k)
            if second:
                for v in range(V):
                    second_part(2 * k, v)
                    second_part(2 * k + 1, v)

    return plane


def section_body(
    state, visc, rims, sector, edges, shared, stencil, out,
    q, nu, rim, edg, fr, ft, axial, res, done, in_sem, misc_sem, out_sem, done_in, done_out,
):
    rest = T - SHARE
    n_chunks = rest // CHUNK
    portion = SHARE // n_chunks

    def fetch(c):
        t0 = c * CHUNK
        return (
            pltpu.make_async_copy(
                state.at[:, pl.ds(SHARE + t0, CHUNK)],
                q.at[:, pl.ds(t0 + 2, CHUNK), pl.ds(TILE, R)],
                in_sem.at[0, c],
            ),
            pltpu.make_async_copy(
                visc.at[pl.ds(SHARE + t0, CHUNK)], nu.at[pl.ds(t0, CHUNK)], in_sem.at[1, c]
            ),
        )

    def fetch_done(c):
        planes = pl.ds(c * portion, portion)
        return pltpu.make_async_copy(shared.at[:, planes], done.at[:, planes], done_in.at[c])

    def send_done(c):
        planes = pl.ds(c * portion, portion)
        return pltpu.make_async_copy(done.at[:, planes], out.at[:, planes], done_out.at[c])

    inner = pl.ds(TILE, R)
    misc = [
        pltpu.make_async_copy(
            state.at[:, pl.ds(SHARE - 2, 2)], q.at[:, pl.ds(0, 2), inner], misc_sem.at[0]
        ),
        pltpu.make_async_copy(sector, q.at[:, pl.ds(rest + 2, 2), inner], misc_sem.at[1]),
        pltpu.make_async_copy(rims.at[:, pl.ds(SHARE, rest)], rim, misc_sem.at[2]),
        pltpu.make_async_copy(edges, edg, misc_sem.at[3]),
    ]
    misc[0].start()
    for copy in fetch(0):
        copy.start()
    for copy in misc[1:]:
        copy.start()
    for c in range(n_chunks):
        fetch_done(c).start()
        if c + 1 < n_chunks:
            for copy in fetch(c + 1):
                copy.start()

    lane = lanes_of()
    edge_lanes = (lane < 2) | (lane >= X - 2)

    def turn_of(t):
        return t // PER, lax.rem(2 * X - 4 - 8 * lax.rem(t, PER), X)

    def insert(turn, v, rows, got):
        edge = pltpu.roll(edg[turn[0], v, rows, :], turn[1], 1)
        return jnp.where(edge_lanes, edge, got)

    plane = plane_maker(
        q, nu, rim, fr, ft, axial, res, stencil, lambda t: turn_of(t + SHARE), insert
    )

    def finish(c):
        fetch_done(c).wait()

        def one(i, carry):
            t = c * portion + i
            turn = turn_of(t)
            for v in range(V):
                for k in range(R // TILE):
                    rows = pl.ds(k * TILE, TILE)
                    done[v, t, rows, :] = insert(turn, v, rows, done[v, t, rows, :])
            return carry

        lax.fori_loop(0, portion, one, 0)
        send_done(c).start()

    def send(t0, count, c):
        return pltpu.make_async_copy(
            res.at[:, pl.ds(t0, count)], out.at[:, pl.ds(SHARE + t0, count)], out_sem.at[c]
        )

    misc[0].wait()
    plane(0, False, False, True, False)
    plane(1, False, False, True, False)
    for copy in fetch(0):
        copy.wait()
    misc[2].wait()
    misc[3].wait()
    for s in range(2, 2 + LAG):
        plane(s, True, False, axial_before=s > 2)
    plane(2 + LAG)

    def steps(low, count):
        def step(i, carry):
            plane(low + i)
            return carry

        lax.fori_loop(0, count, step, 0)

    steps(3 + LAG, CHUNK - 1 - LAG)
    send(0, CHUNK - LAG, 0).start()
    finish(0)

    def chunk(c, carry):
        for copy in fetch(c):
            copy.wait()
        steps(c * CHUNK + 2, CHUNK)
        send(c * CHUNK - LAG, CHUNK, c).start()
        finish(c)
        return carry

    lax.fori_loop(1, n_chunks, chunk, 0)
    misc[1].wait()
    plane(rest + 2, False, True, True)
    plane(rest + 3, False, True, True, False)
    plane(rest + 4, False, True, False, False)
    send(rest - LAG, LAG, n_chunks).start()
    send(0, CHUNK - LAG, 0).wait()

    def drain(c, carry):
        send(c * CHUNK - LAG, CHUNK, c).wait()
        return carry

    lax.fori_loop(1, n_chunks, drain, 0)
    send(rest - LAG, LAG, n_chunks).wait()
    for c in range(n_chunks):
        send_done(c).wait()


def section_call(state, visc, rims, sector, edges, shared, stencil):
    any_space = pl.BlockSpec(memory_space=pl.ANY)
    f32 = jnp.float32
    rest = T - SHARE
    dma = pltpu.SemaphoreType.DMA
    return pl.pallas_call(
        section_body,
        out_shape=jax.ShapeDtypeStruct((V, T, R, X), f32),
        in_specs=[any_space] * 6 + [pl.BlockSpec(memory_space=pltpu.VMEM)],
        out_specs=any_space,
        scratch_shapes=[
            pltpu.VMEM((V, rest + 5, PAD, X), f32),
            pltpu.VMEM((rest, R, X), f32),
            pltpu.VMEM((V, rest, 4, X), f32),
            pltpu.VMEM((GROUPS, V, R, X), f32),
            pltpu.VMEM((V - 1, rest, PAD, X), f32),
            pltpu.VMEM((V - 1, rest + 5, R, X), f32),
            pltpu.VMEM((V, R, 2 * X), jnp.bfloat16),
            pltpu.VMEM((V, rest, R, X), f32),
            pltpu.VMEM((V, SHARE, R, X), f32),
            dma((2, rest // CHUNK)),
            dma((4,)),
            dma((rest // CHUNK + 1,)),
            dma((rest // CHUNK,)),
            dma((rest // CHUNK,)),
        ],
        compiler_params=pltpu.CompilerParams(vmem_limit_bytes=60 * 1024 * 1024),
        cost_estimate=pl.CostEstimate(
            flops=150 * rest * R * X, bytes_accessed=24_000_000, transcendentals=rest * R * X
        ),
    )(state, visc, rims, sector, edges, shared, stencil)


def spread_table(columns):
    table = np.zeros((GROUPS * X, len(columns) * X), np.float32)
    for place, j in enumerate(columns):
        for t in range(T):
            group, slot = divmod(t, PER)
            for side in range(2):
                e = 4 + j if side == 0 else 3 - j
                table[group * X + slot * 8 + e, place * X + side * T + t] = 1
    return table


def halo_table():
    table = np.zeros((X, 4 * X), np.float32)
    for j in range(2):
        for side in range(2):
            e = 4 + j if side == 0 else 3 - j
            for slot, lane in ((1, 0), (2, T - 1)):
                table[slot * 8 + e, 2 * j * X + side * T + lane] = 1
            for slot, lane in ((0, 0), (1, 1), (2, T - 2), (3, T - 1)):
                table[slot * 8 + e, (2 * j + 1) * X + side * T + lane] = 1
    return table


def exact_dot(x, table):
    high, low = split(x)
    return dot(high, table) + dot(low, table)


def sine(n):
    rest = n & 1023
    folded = jnp.minimum(rest, 1024 - rest).astype(jnp.float32) * (math.pi / 1024)
    s = folded * folded
    p = jnp.float32(-2.5052108e-08)
    for c in (2.7557319e-06, -1.9841270e-04, 8.3333333e-03, -1.6666667e-01, 1.0):
        p = p * s + c
    p = p * folded
    return jnp.where(n < 1024, p, -p)


PARTS = (2 + LAG, 12, 24, SHARE + LAG + 2)


def edges_body(
    n_theta, n_ax,
    state, visc, rims, spread, place, halo, stencil, coupling, block_map, plane_flags, cutoff,
    edges, sector, shared,
    q, nu, rim, fr, ft, axial, out, tabs, tabp, tabh, packed, packed_hal, edge, around, ax_out, ax_in,
    rad, sect, send_a, recv_a, send_b, recv_b, gh, gl, lhs, filt, res,
    in_sem, misc_sem, halo_send, halo_recv, ax_send, ax_recv, a_send, a_recv, b_send, b_recv, out_sem,
):
    me = lax.axis_index("theta")
    my_ax = lax.axis_index("ax")
    nxt, prv = lax.rem(me + 1, n_theta), lax.rem(me + n_theta - 1, n_theta)
    right, left = lax.rem(my_ax + 1, n_ax), lax.rem(my_ax + n_ax - 1, n_ax)
    rs = R // n_theta

    def fetch(g):
        return pltpu.make_async_copy(
            state.at[:, pl.ds(g * PER, PER)],
            q.at[:, pl.ds(2 + g * PER, PER), pl.ds(TILE, R)],
            in_sem.at[g],
        )

    misc = [
        pltpu.make_async_copy(rims, rim, misc_sem.at[0]),
        pltpu.make_async_copy(visc, nu, misc_sem.at[1]),
        pltpu.make_async_copy(spread, tabs, misc_sem.at[2]),
        pltpu.make_async_copy(place, tabp, misc_sem.at[3]),
        pltpu.make_async_copy(halo, tabh, misc_sem.at[4]),
    ]
    for g in range(GROUPS):
        fetch(g).start()
    for copy in misc:
        copy.start()

    barrier = pltpu.get_barrier_semaphore()

    def greet(i, carry):
        pl.semaphore_signal(
            barrier, inc=1, device_id=(lax.rem(me + i, n_theta), my_ax), device_id_type=MESH
        )
        return carry

    lax.fori_loop(1, n_theta, greet, 0)
    for other in (left, right):
        pl.semaphore_signal(barrier, inc=1, device_id=(me, other), device_id_type=MESH)
    twice = 2 * cutoff[0] - 1

    def weights(b, carry):
        def some(i, carry):
            rows = pl.ds(pl.multiple_of(i * 16, 16), 16)
            down = lax.broadcasted_iota(jnp.int32, (16, 256), 0) + i * 16
            along = lax.broadcasted_iota(jnp.int32, (16, 256), 1)
            tau = (b * 256 + along - down) & 1023
            top = sine((twice * tau) & 2047)
            below = sine(jnp.maximum(tau, 1))
            ratio = jnp.where(tau == 0, twice.astype(jnp.float32), top / below)
            g = (ratio - 1.0) * (1.0 / 1024)
            high, low = split(g)
            gh[b, rows, :] = high
            gl[b, rows, :] = low
            return carry

        return lax.fori_loop(0, 16, some, carry)

    lax.fori_loop(0, 4, weights, 0)

    pl.semaphore_wait(barrier, n_theta + 1)

    def to_sector(i, cells, peer):
        return pltpu.make_async_remote_copy(
            src_ref=state.at[:, cells],
            dst_ref=q.at[:, pl.ds(i * (T + 2), 2), pl.ds(TILE, R)],
            send_sem=halo_send.at[i],
            recv_sem=halo_recv.at[i],
            device_id=(peer, my_ax),
            device_id_type=MESH,
        )

    halos = [to_sector(0, pl.ds(T - 2, 2), nxt), to_sector(1, pl.ds(0, 2), prv)]
    for copy in halos:
        copy.start()

    lane = lanes_of()
    slot_of = lane // 8

    def pack(load, slots):
        acc = None
        for slot in range(slots):
            turned = pltpu.roll(load(slot), (8 * slot + 4) % X, 1)
            if acc is None:
                acc = turned
            else:
                acc = jnp.where(slot_of[: turned.shape[0]] == slot, turned, acc)
        return acc

    for v in range(V + 1):
        packed[v, pl.ds(R, TILE), :] = jnp.zeros((TILE, GROUPS * X), jnp.float32)
    misc[0].wait()
    misc[1].wait()
    for g in range(GROUPS):
        cols = pl.ds(g * X, X)
        for v in range(V):
            packed[v, pl.ds(R, 4), cols] = pack(lambda t: rim[v, g * PER + t], PER)
    for g in range(GROUPS):
        fetch(g).wait()
        cols = pl.ds(g * X, X)

        def rows_of(k, carry):
            rows = pl.ds(pl.multiple_of(k * TILE, TILE), TILE)
            wide = pl.ds(pl.multiple_of(k * TILE + TILE, TILE), TILE)
            for v in range(V):
                packed[v, rows, cols] = pack(lambda t: q[v, 2 + g * PER + t, wide, :], PER)
            packed[V, rows, cols] = pack(lambda t: nu[g * PER + t, rows, :], PER)
            return carry

        lax.fori_loop(0, R // TILE, rows_of, 0)
    for copy in misc[2:]:
        copy.wait()

    def unpack(v, carry):
        got = exact_dot(packed[v, pl.ds(0, R + TILE), :], tabs[...])
        for j in range(4):
            edge[j, v] = got[:, j * X : (j + 1) * X]
        return carry

    lax.fori_loop(0, V + 1, unpack, 0)

    first = lane < T

    def stage(k, carry):
        rows = pl.ds(pl.multiple_of(k * TILE, TILE), TILE)
        for v in range(V):
            near, far = edge[0, v, rows, :], edge[1, v, rows, :]
            ax_out[0, v, rows, :] = jnp.where(first, near, roll(far, T))
            ax_out[1, v, rows, :] = jnp.where(first, roll(near, T), far)
        return carry

    lax.fori_loop(0, R // TILE, stage, 0)

    def to_ax(i, peer):
        return pltpu.make_async_remote_copy(
            src_ref=ax_out.at[i],
            dst_ref=ax_in.at[i],
            send_sem=ax_send.at[i],
            recv_sem=ax_recv.at[i],
            device_id=(me, peer),
            device_id_type=MESH,
        )

    sides = [to_ax(0, left), to_ax(1, right)]
    for copy in sides:
        copy.start()

    for copy in halos:
        copy.wait_recv()

    def pack_halo(k, carry):
        rows = pl.ds(pl.multiple_of(k * TILE, TILE), TILE)
        wide = pl.ds(pl.multiple_of(k * TILE + TILE, TILE), TILE)
        for v in range(V):
            packed_hal[v, rows, :] = pack(lambda t: q[v, t + T * (t // 2), wide, :], 4)
        return carry

    lax.fori_loop(0, R // TILE, pack_halo, 0)

    def unpack_halo(v, carry):
        got = exact_dot(packed_hal[v], tabh[...])
        for i in range(4):
            around[i, v] = got[:, i * X : (i + 1) * X]
        return carry

    lax.fori_loop(0, V, unpack_halo, 0)

    to_hbm = [
        pltpu.make_async_copy(
            q.at[:, pl.ds(T + 2, 2), pl.ds(TILE, R)], sector, out_sem.at[0]
        )
    ]
    to_hbm[0].start()

    def radial(k, carry):
        rows = pl.ds(pl.multiple_of(k * TILE, TILE), TILE)
        wide = pl.ds(pl.multiple_of(k * TILE + TILE, TILE), TILE)
        for j in range(2):
            cell = [edge[j, v, rows, :] for v in range(V)]
            f = flux_r(cell, velocities(cell))
            for v in range(V):
                rad[j, v, wide, :] = f[v]
                rad[j, V + v, wide, :] = cell[v]
        return carry

    lax.fori_loop(0, R // TILE, radial, 0)
    for j in range(2):
        cell = [edge[j, v, pl.ds(R, TILE), :] for v in range(V)]
        f = flux_r(cell, velocities(cell))
        for v in range(V):
            for i, kept in ((v, f[v]), (V + v, cell[v])):
                rad[j, i, pl.ds(TILE - 2, 2), :] = kept[0:2]
                rad[j, i, pl.ds(TILE + R, 2), :] = kept[2:4]

    plane = plane_maker(q, nu, rim, fr, ft, axial, out, stencil)

    def planes(part):
        low, high = PARTS[part], PARTS[part + 1]

        def step(s, carry):
            plane(s)
            return carry

        lax.fori_loop(low, high, step, 0)
        t0, t1 = (0 if part == 0 else low - 2 - LAG), high - 2 - LAG
        copy = pltpu.make_async_copy(
            out.at[:, pl.ds(t0, t1 - t0)], shared.at[:, pl.ds(t0, t1 - t0)], out_sem.at[2 + part]
        )
        copy.start()
        to_hbm.append(copy)

    plane(0, False, False, True, False)
    plane(1, False, False, True, False)
    for s in range(2, 2 + LAG):
        plane(s, True, False, axial_before=s > 2)
    planes(0)

    for copy in sides:
        copy.wait_recv()

    sign = jnp.where(first, 1.0, -1.0).astype(jnp.float32)
    has_left = (my_ax > 0).astype(jnp.int32)
    has_right = (my_ax < n_ax - 1).astype(jnp.int32)
    inside = jnp.where(first, has_left, has_right) == 1
    at = lane & (T - 1)

    def section(k, carry):
        rows = pl.ds(pl.multiple_of(k * TILE, TILE), TILE)
        low = pl.multiple_of(k * TILE, TILE)
        cells, fluxes = {}, {}
        for j in range(-2, 4):
            if j >= 0:
                cell = [edge[j, v, rows, :] for v in range(V)]
            else:
                cell = []
                for v in range(V):
                    a, b = ax_in[1, v, rows, :], ax_in[0, v, rows, :]
                    if j == -1:
                        cell.append(jnp.where(first, a, roll(b, T)))
                    else:
                        cell.append(jnp.where(first, roll(a, T), b))
            vel = velocities(cell)
            f = flux_x(cell, vel)
            if j < 0:
                f = [jnp.where(inside, x, 0.0) for x in f]
                cell = [jnp.where(inside, x, 0.0) for x in cell]
            cells[j], fluxes[j] = cell, f
        for j in range(2):
            cell = cells[j]
            f = flux_t(cell, velocities(cell))
            halo_cell = [[around[2 * j + i, v, rows, :] for v in range(V)] for i in range(2)]
            halo_flux = [flux_t(c, velocities(c)) for c in halo_cell]
            n = edge[j, V, rows, :]
            n12 = 12.0 * n
            kq = 60.0 - 72.0 * n
            for v in range(V):

                def step(o, own, near, far):
                    ends = (at >= T - o) if o > 0 else (at < -o)
                    return jnp.where(ends, near if abs(o) == 1 else far, roll(own, -o))

                def cir(o):
                    return step(o, f[v], halo_flux[0][v], halo_flux[1][v])

                def cir_cell(o):
                    return step(o, cell[v], halo_cell[0][v], halo_cell[1][v])

                def r_at(i, o):
                    return rad[j, i, pl.ds(low + TILE + o, TILE), :]

                axial = 8.0 * (fluxes[j + 1][v] - fluxes[j - 1][v]) - (
                    fluxes[j + 2][v] - fluxes[j - 2][v]
                )
                near = (r_at(v, 1) - r_at(v, -1)) + (cir(1) - cir(-1))
                far = (r_at(v, 2) - r_at(v, -2)) + (cir(2) - cir(-2))
                side = (
                    (cells[j + 1][v] + cells[j - 1][v])
                    + (r_at(V + v, 1) + r_at(V + v, -1))
                    + (cir_cell(1) + cir_cell(-1))
                )
                sect[j, v, rows, :] = UNIT * (
                    kq * cell[v] + n12 * side - sign * axial - 8.0 * near + far
                )
        return carry

    lax.fori_loop(0, R // TILE, section, 0)

    for d in range(n_theta):
        send_a[d, pl.ds(V * rs, ROWS - V * rs), :] = jnp.zeros((ROWS - V * rs, X), jnp.float32)
        for v in range(V):
            send_a[d, pl.ds(v * rs, rs), :] = sect[0, v, pl.ds(d * rs, rs), :]

    def block_copy(src, dst, sems, i):
        peer = lax.rem(me + i, n_theta)
        return pltpu.make_async_remote_copy(
            src_ref=src.at[peer],
            dst_ref=dst.at[me],
            send_sem=sems[0].at[i],
            recv_sem=sems[1].at[i],
            device_id=(peer, my_ax),
            device_id_type=MESH,
        )

    def start_all(src, dst, sems):
        def go(i, carry):
            block_copy(src, dst, sems, i).start()
            return carry

        lax.fori_loop(1, n_theta, go, 0)

    def finish_all(src, dst, sems):
        def go(i, carry):
            block_copy(src, dst, sems, i).wait()
            return carry

        lax.fori_loop(1, n_theta, go, 0)

    start_all(send_a, recv_a, (a_send, a_recv))
    recv_a[me] = send_a[me]
    planes(1)
    finish_all(send_a, recv_a, (a_send, a_recv))

    wide_first = lanes_of(ROWS) < T
    for s in range(n_theta // 2):
        a, b = recv_a[2 * s], recv_a[2 * s + 1]
        cols = pl.ds(s * X, X)
        both = [jnp.where(wide_first, a, roll(b, T)), jnp.where(wide_first, roll(a, T), b)]
        for i in range(2):
            high, low = split(both[i])
            lhs[pl.ds(i * ROWS, ROWS), cols] = high.astype(jnp.float32)
            lhs[pl.ds((2 + i) * ROWS, ROWS), cols] = low.astype(jnp.float32)

    blocks = n_theta * T // 256
    terms = [lhs[:, a * 256 : (a + 1) * 256].astype(jnp.bfloat16) for a in range(blocks)]
    for b in range(blocks):
        total = None
        for a in range(blocks):
            k = (b - a) % blocks
            wide = dot(terms[a], gh[k])
            term = (wide[: 2 * ROWS] + wide[2 * ROWS :]) + dot(terms[a][: 2 * ROWS], gl[k])
            total = term if total is None else total + term
        filt[:, b * 256 : (b + 1) * 256] = total

    for s in range(n_theta // 2):
        cols = pl.ds(s * X, X)
        a, b = filt[pl.ds(0, ROWS), cols], filt[pl.ds(ROWS, ROWS), cols]
        send_b[2 * s] = jnp.where(wide_first, a, roll(b, T))
        send_b[2 * s + 1] = jnp.where(wide_first, roll(a, T), b)

    start_all(send_b, recv_b, (b_send, b_recv))
    recv_b[me] = send_b[me]
    planes(2)
    finish_all(send_b, recv_b, (b_send, b_recv))

    flag = plane_flags[block_map[my_ax]]
    on = jnp.where(lanes_of(rs) < T, lax.rem(flag, 2), lax.div(flag, 2)) == 1
    for d in range(n_theta):
        mode = [recv_b[d, pl.ds(v * rs, rs), :] for v in range(V)]
        for u in range(V):
            added = coupling[u, 0] * mode[0]
            for v in range(1, V):
                added += coupling[u, v] * mode[v]
            rows = pl.ds(d * rs, rs)
            own = sect[0, u, rows, :]
            sect[0, u, rows, :] = jnp.where(on, own + added, own)

    for v in range(V):
        both = jnp.concatenate([sect[0, v], sect[1, v]], axis=1)
        got = exact_dot(both, tabp[...])
        for g in range(GROUPS):
            res[g, v] = got[:, g * X : (g + 1) * X]
    to_hbm.append(pltpu.make_async_copy(res, edges, out_sem.at[1]))
    to_hbm[-1].start()
    for copy in halos + sides:
        copy.wait_send()
    for copy in to_hbm:
        copy.wait()


def edges_call(mesh, state, visc, rims, stencil, coupling, block_map, plane_flags, cutoff):
    n_theta, n_ax = mesh.shape["theta"], mesh.shape["ax"]
    any_space = pl.BlockSpec(memory_space=pl.ANY)
    smem = pl.BlockSpec(memory_space=pltpu.SMEM)
    f32, bf16 = jnp.float32, jnp.bfloat16
    tabs = spread_table(range(4))
    tables = [jnp.asarray(x, bf16) for x in (tabs, tabs[:, : 2 * X].T, halo_table())]
    dma = pltpu.SemaphoreType.DMA
    return pl.pallas_call(
        functools.partial(edges_body, n_theta, n_ax),
        out_shape=(
            jax.ShapeDtypeStruct((GROUPS, V, R, X), f32),
            jax.ShapeDtypeStruct((V, 2, R, X), f32),
            jax.ShapeDtypeStruct((V, SHARE, R, X), f32),
        ),
        in_specs=[any_space] * 6 + [pl.BlockSpec(memory_space=pltpu.VMEM)] + [smem] * 4,
        out_specs=(any_space, any_space, any_space),
        scratch_shapes=[
            pltpu.VMEM((V, T + 4, PAD, X), f32),
            pltpu.VMEM((T, R, X), f32),
            pltpu.VMEM((V, T, 4, X), f32),
            pltpu.VMEM((V - 1, SHARE + LAG, PAD, X), f32),
            pltpu.VMEM((V - 1, SHARE + LAG + 2, R, X), f32),
            pltpu.VMEM((V, R, 2 * X), bf16),
            pltpu.VMEM((V, SHARE + LAG, R, X), f32),
            pltpu.VMEM((GROUPS * X, 4 * X), bf16),
            pltpu.VMEM((2 * X, GROUPS * X), bf16),
            pltpu.VMEM((X, 4 * X), bf16),
            pltpu.VMEM((V + 1, R + TILE, GROUPS * X), f32),
            pltpu.VMEM((V, R, X), f32),
            pltpu.VMEM((4, V + 1, R + TILE, X), f32),
            pltpu.VMEM((4, V, R, X), f32),
            pltpu.VMEM((2, V, R, X), f32),
            pltpu.VMEM((2, V, R, X), f32),
            pltpu.VMEM((2, 2 * V, PAD, X), f32),
            pltpu.VMEM((2, V, R, X), f32),
            pltpu.VMEM((n_theta, ROWS, X), f32),
            pltpu.VMEM((n_theta, ROWS, X), f32),
            pltpu.VMEM((n_theta, ROWS, X), f32),
            pltpu.VMEM((n_theta, ROWS, X), f32),
            pltpu.VMEM((4, 256, 256), bf16),
            pltpu.VMEM((4, 256, 256), bf16),
            pltpu.VMEM((4 * ROWS, n_theta * T), f32),
            pltpu.VMEM((2 * ROWS, n_theta * T), f32),
            pltpu.VMEM((GROUPS, V, R, X), f32),
            dma((GROUPS,)),
            dma((5,)),
            dma((2,)),
            dma((2,)),
            dma((2,)),
            dma((2,)),
            dma((n_theta,)),
            dma((n_theta,)),
            dma((n_theta,)),
            dma((n_theta,)),
            dma((5,)),
        ],
        compiler_params=pltpu.CompilerParams(
            collective_id=0, has_side_effects=True, vmem_limit_bytes=60 * 1024 * 1024
        ),
        cost_estimate=pl.CostEstimate(
            flops=400_000_000, bytes_accessed=14_000_000, transcendentals=0
        ),
    )(state, visc, rims, *tables, stencil, coupling, block_map, plane_flags, cutoff)


def solution(mesh):
    def local(state, viscosity, band_rims, coupling, block_map, plane_flags, mode_cutoff):
        stencil = jnp.asarray(stencil_table(), jnp.bfloat16)
        edges, sector, shared = edges_call(
            mesh,
            state,
            viscosity,
            band_rims,
            stencil,
            coupling,
            block_map,
            plane_flags,
            mode_cutoff,
        )
        return section_call(state, viscosity, band_rims, sector, edges, shared, stencil)

    in_specs = (
        P(None, "theta", None, "ax"),
        P("theta", None, "ax"),
        P(None, "theta", None, "ax"),
        P(),
        P(),
        P(),
        P(),
    )
    out_specs = P(None, "theta", None, "ax")
    return jax.shard_map(local, mesh=mesh, in_specs=in_specs, out_specs=out_specs, check_vma=False)
```

time: 70 us -> 57.5 us (0.82)
  Pallas kernels: 69.2 us -> 56.6 us
    pallas_call x1, Pallas kernels: 29.8 us -> 16.2 us  [section_call(): pl.pallas_call(section_body, out_shape=jax.ShapeDtypeStruct((V, T, R, X),...]
    pallas_call x1, Pallas kernels: 39.5 us -> 40.4 us  [edges_call(): pl.pallas_call(functools.partial(edges_body, n_theta, n_ax), out_shape=(j...]
where the time goes in v1:
time: 57.5 us; the launch traced here: 57.3 us
  Pallas kernels  56.6 us (98%)
  between operations  0.66 us (1%)
    pallas_call x1, Pallas kernels, edges_call(): pl.pallas_call(functools.partial(edges_body, n_theta, n_ax), out_shape=(j...  40.4 us
    pallas_call x1, Pallas kernels, section_call(): pl.pallas_call(section_body, out_shape=jax.ShapeDtypeStruct((V, T, R, X),...  16.2 us

profile of v1, /device:TPU:1, one launch (start us, length us, event | category | flops | bytes accessed | tf_op | source)
XLA Modules:
  0.0 57.3 jit_solution(17079592925119124098)
XLA Ops:
  0.7 40.4 %shard_map.109 = (f32[4,5,64,128]{3,2,1,0:T(8,128)}, f32[5,2,64,128]{3,2,1,0:T(8,128)}, f32[5,32,64,128]{3,2,1,0:T(8,128)}) custom-call(f32[5,64,64,128]{3,2,1,0:T(8,128)} %state.3, f32[64,64,128]{2,1,0:T(8,128)} %visc.3, f32[5,64,4,128]{3,2,1,0:T(4,128)} %rims.3, bf16[512,512]{1,0:T(8,128)(2,1)} %constant.9.clone.spread, ...), custom_call_target="tpu_custom_call" | custom-call | flops 400000000 | bytes 14000000 | tf_op jit(solution)/shard_map/pallas_call | solution.py:787
  41.1 16.2 %shard_map.110 = f32[5,64,64,128]{3,2,1,0:T(8,128)} custom-call(f32[5,64,64,128]{3,2,1,0:T(8,128)} %state.3, f32[64,64,128]{2,1,0:T(8,128)} %visc.3, f32[5,64,4,128]{3,2,1,0:T(4,128)} %rims.3, f32[5,2,64,128]{3,2,1,0:T(8,128)} %get-tuple-element.8.sector, f32[4,5,64,128]{3,2,1,0:T(8,128)} %get-tuple-element.9.edges, ...), custom_call_target="tpu_custom_call" | custom-call | flops 39321600 | bytes 24000000 | tf_op jit(solution)/shard_map/pallas_call | solution.py:325

commit v2 on v1

--- a/solution.py
+++ b/solution.py
@@ -19,7 +19,7 @@
 GROUPS = 4
 PER = 16
 CHUNK = 8
-SHARE = 32
+SHARE = 40
 LAG = 3
 ROWS = 24
 MESH = pl.DeviceIdType.MESH
@@ -192,7 +192,6 @@
 ):
     rest = T - SHARE
     n_chunks = rest // CHUNK
-    portion = SHARE // n_chunks
 
     def fetch(c):
         t0 = c * CHUNK
@@ -207,12 +206,17 @@
             ),
         )
 
-    def fetch_done(c):
-        planes = pl.ds(c * portion, portion)
+    head = CHUNK - 1 - LAG
+    each = SHARE // (rest - CHUNK + head)
+    portions = [(0, head * each)]
+    portions += [((head + CHUNK * (c - 1)) * each, CHUNK * each) for c in range(1, n_chunks)]
+
+    def fetch_part(t0, count, c):
+        planes = pl.ds(t0, count)
         return pltpu.make_async_copy(shared.at[:, planes], done.at[:, planes], done_in.at[c])
 
-    def send_done(c):
-        planes = pl.ds(c * portion, portion)
+    def send_part(t0, count, c):
+        planes = pl.ds(t0, count)
         return pltpu.make_async_copy(done.at[:, planes], out.at[:, planes], done_out.at[c])
 
     inner = pl.ds(TILE, R)
@@ -225,15 +229,16 @@
         pltpu.make_async_copy(edges, edg, misc_sem.at[3]),
     ]
     misc[0].start()
+    misc[2].start()
     for copy in fetch(0):
         copy.start()
-    for copy in misc[1:]:
-        copy.start()
-    for c in range(n_chunks):
-        fetch_done(c).start()
-        if c + 1 < n_chunks:
-            for copy in fetch(c + 1):
-                copy.start()
+    misc[3].start()
+    fetch_part(*portions[0], 0).start()
+    for c in range(1, n_chunks):
+        for copy in fetch(c):
+            copy.start()
+        fetch_part(*portions[c], c).start()
+    misc[1].start()
 
     lane = lanes_of()
     edge_lanes = (lane < 2) | (lane >= X - 2)
@@ -249,20 +254,13 @@
         q, nu, rim, fr, ft, axial, res, stencil, lambda t: turn_of(t + SHARE), insert
     )
 
-    def finish(c):
-        fetch_done(c).wait()
-
-        def one(i, carry):
-            t = c * portion + i
-            turn = turn_of(t)
-            for v in range(V):
-                for k in range(R // TILE):
-                    rows = pl.ds(k * TILE, TILE)
-                    done[v, t, rows, :] = insert(turn, v, rows, done[v, t, rows, :])
-            return carry
-
-        lax.fori_loop(0, portion, one, 0)
-        send_done(c).start()
+    def finish(t):
+        turn = turn_of(t)
+        near = done.at[:, pl.ds(t, 1)]
+        for v in range(V):
+            for k in range(R // TILE):
+                rows = pl.ds(k * TILE, TILE)
+                near[v, 0, rows, :] = insert(turn, v, rows, near[v, 0, rows, :])
 
     def send(t0, count, c):
         return pltpu.make_async_copy(
@@ -272,49 +270,53 @@
     misc[0].wait()
     plane(0, False, False, True, False)
     plane(1, False, False, True, False)
+    misc[2].wait()
     for copy in fetch(0):
         copy.wait()
-    misc[2].wait()
-    misc[3].wait()
     for s in range(2, 2 + LAG):
         plane(s, True, False, axial_before=s > 2)
+    misc[3].wait()
     plane(2 + LAG)
 
     def steps(low, count):
         def step(i, carry):
             plane(low + i)
+            for j in range(each):
+                finish((low + i - 3 - LAG) * each + j)
             return carry
 
         lax.fori_loop(0, count, step, 0)
 
-    steps(3 + LAG, CHUNK - 1 - LAG)
+    fetch_part(*portions[0], 0).wait()
+    steps(3 + LAG, head)
     send(0, CHUNK - LAG, 0).start()
-    finish(0)
+    send_part(*portions[0], 0).start()
 
     def chunk(c, carry):
         for copy in fetch(c):
             copy.wait()
+        t0 = (head + CHUNK * (c - 1)) * each
+        fetch_part(t0, CHUNK * each, c).wait()
         steps(c * CHUNK + 2, CHUNK)
         send(c * CHUNK - LAG, CHUNK, c).start()
-        finish(c)
+        send_part(t0, CHUNK * each, c).start()
         return carry
 
     lax.fori_loop(1, n_chunks, chunk, 0)
     misc[1].wait()
-    plane(rest + 2, False, True, True)
-    plane(rest + 3, False, True, True, False)
-    plane(rest + 4, False, True, False, False)
+    for i in range(LAG):
+        plane(rest + 2 + i, False, True, i < 2, i < 1)
     send(rest - LAG, LAG, n_chunks).start()
     send(0, CHUNK - LAG, 0).wait()
 
     def drain(c, carry):
         send(c * CHUNK - LAG, CHUNK, c).wait()
+        send_part((head + CHUNK * (c - 1)) * each, CHUNK * each, c).wait()
         return carry
 
     lax.fori_loop(1, n_chunks, drain, 0)
+    send_part(*portions[0], 0).wait()
     send(rest - LAG, LAG, n_chunks).wait()
-    for c in range(n_chunks):
-        send_done(c).wait()
 
 
 def section_call(state, visc, rims, sector, edges, shared, stencil):
@@ -361,6 +363,14 @@
     return table
 
 
+def pick_table():
+    table = np.zeros((PER, 2, X, X), np.float32)
+    for slot in range(PER):
+        for e in range(8):
+            table[slot, :, (X - 4 + e) % X, slot * 8 + e] = 1
+    return table.reshape(PER // 2, 4 * X, X)
+
+
 def halo_table():
     table = np.zeros((X, 4 * X), np.float32)
     for j in range(2):
@@ -389,16 +399,16 @@
     return jnp.where(n < 1024, p, -p)
 
 
-PARTS = (2 + LAG, 12, 24, SHARE + LAG + 2)
+PARTS = (4 + LAG, 17, 31, SHARE + LAG + 2)
 
 
 def edges_body(
     n_theta, n_ax,
-    state, visc, rims, spread, place, halo, stencil, coupling, block_map, plane_flags, cutoff,
+    state, visc, rims, spread, place, halo, pick, stencil, coupling, block_map, plane_flags, cutoff,
     edges, sector, shared,
-    q, nu, rim, fr, ft, axial, out, tabs, tabp, tabh, packed, packed_hal, edge, around, ax_out, ax_in,
+    q, nu, rim, fr, ft, axial, out, tabs, tabp, tabh, tabk, packed, packed_hal, rim_out, rim_in, edge, around, ax_out, ax_in,
     rad, sect, send_a, recv_a, send_b, recv_b, gh, gl, lhs, filt, res,
-    in_sem, misc_sem, halo_send, halo_recv, ax_send, ax_recv, a_send, a_recv, b_send, b_recv, out_sem,
+    in_sem, misc_sem, rim_send, rim_recv, halo_send, halo_recv, ax_send, ax_recv, a_send, a_recv, b_send, b_recv, out_sem,
 ):
     me = lax.axis_index("theta")
     my_ax = lax.axis_index("ax")
@@ -419,10 +429,13 @@
         pltpu.make_async_copy(spread, tabs, misc_sem.at[2]),
         pltpu.make_async_copy(place, tabp, misc_sem.at[3]),
         pltpu.make_async_copy(halo, tabh, misc_sem.at[4]),
+        pltpu.make_async_copy(pick, tabk, misc_sem.at[5]),
     ]
+    for copy in misc[:2] + misc[5:]:
+        copy.start()
     for g in range(GROUPS):
         fetch(g).start()
-    for copy in misc:
+    for copy in misc[2:5]:
         copy.start()
 
     barrier = pltpu.get_barrier_semaphore()
@@ -494,29 +507,42 @@
         cols = pl.ds(g * X, X)
         for v in range(V):
             packed[v, pl.ds(R, 4), cols] = pack(lambda t: rim[v, g * PER + t], PER)
-    for g in range(GROUPS):
+    misc[5].wait()
+
+    def group(g, carry):
         fetch(g).wait()
-        cols = pl.ds(g * X, X)
-
-        def rows_of(k, carry):
-            rows = pl.ds(pl.multiple_of(k * TILE, TILE), TILE)
-            wide = pl.ds(pl.multiple_of(k * TILE + TILE, TILE), TILE)
-            for v in range(V):
-                packed[v, rows, cols] = pack(lambda t: q[v, 2 + g * PER + t, wide, :], PER)
-            packed[V, rows, cols] = pack(lambda t: nu[g * PER + t, rows, :], PER)
-            return carry
-
-        lax.fori_loop(0, R // TILE, rows_of, 0)
-    for copy in misc[2:]:
+        cols = pl.ds(pl.multiple_of(g * X, X), X)
+        tiles = [(v, k) for v in (3, 4, 5) for k in range(R // TILE)]
+        total = None
+        for two in range(PER // 2):
+            tall = []
+            for v in (0, 1, 2):
+                wide = []
+                for slot in (2 * two, 2 * two + 1):
+                    wide += split(q[v, 2 + g * PER + slot, pl.ds(TILE, R), :])
+                tall.append(jnp.concatenate(wide, axis=1))
+            term = dot(jnp.concatenate(tall, axis=0), tabk[two])
+            total = term if total is None else total + term
+            for v, k in tiles[3 * two : 3 * two + 3]:
+                rows, wide = pl.ds(k * TILE, TILE), pl.ds(k * TILE + TILE, TILE)
+                if v < V:
+                    packed[v, rows, cols] = pack(lambda t: q[v, 2 + g * PER + t, wide, :], PER)
+                else:
+                    packed[v, rows, cols] = pack(lambda t: nu[g * PER + t, rows, :], PER)
+        for v in range(3):
+            packed[v, pl.ds(0, R), cols] = total[v * R : (v + 1) * R]
+        return carry
+
+    lax.fori_loop(0, GROUPS, group, 0)
+    for copy in misc[2:5]:
         copy.wait()
 
-    def unpack(v, carry):
-        got = exact_dot(packed[v, pl.ds(0, R + TILE), :], tabs[...])
-        for j in range(4):
-            edge[j, v] = got[:, j * X : (j + 1) * X]
-        return carry
-
-    lax.fori_loop(0, V + 1, unpack, 0)
+    high = R + TILE
+    for some in (pl.ds(0, 3), pl.ds(3, 3)):
+        got = exact_dot(packed[some].reshape(3 * high, GROUPS * X), tabs[...])
+        for i in range(3):
+            for j in range(4):
+                edge[j, some.start + i] = got[i * high : (i + 1) * high, j * X : (j + 1) * X]
 
     first = lane < T
 
@@ -541,35 +567,49 @@
         )
 
     sides = [to_ax(0, left), to_ax(1, right)]
-    for copy in sides:
+    has_left, has_right = my_ax > 0, my_ax < n_ax - 1
+
+    @pl.when(has_left)
+    def _():
+        sides[0].start()
+
+    @pl.when(has_right)
+    def _():
+        sides[1].start()
+
+    @pl.when(jnp.logical_not(has_left))
+    def _():
+        ax_in[1] = ax_out[0]
+
+    @pl.when(jnp.logical_not(has_right))
+    def _():
+        ax_in[0] = ax_out[0]
+
+    block_of = lane // (2 * TILE)
+    for v in range(V):
+        for i, cols, start in ((0, (GROUPS - 1) * X, X - 2 * TILE), (1, 0, 0)):
+            acc = None
+            for k in range(R // TILE):
+                own = packed[v, pl.ds(k * TILE, TILE), pl.ds(cols, X)]
+                turned = roll(own, 2 * TILE * k - start)
+                acc = turned if acc is None else jnp.where(block_of == k, turned, acc)
+            rim_out[i, v] = acc
+
+    def to_rim(i, peer):
+        return pltpu.make_async_remote_copy(
+            src_ref=rim_out.at[i],
+            dst_ref=rim_in.at[i],
+            send_sem=rim_send.at[i],
+            recv_sem=rim_recv.at[i],
+            device_id=(peer, my_ax),
+            device_id_type=MESH,
+        )
+
+    ends = [to_rim(0, nxt), to_rim(1, prv)]
+    for copy in ends:
         copy.start()
 
-    for copy in halos:
-        copy.wait_recv()
-
-    def pack_halo(k, carry):
-        rows = pl.ds(pl.multiple_of(k * TILE, TILE), TILE)
-        wide = pl.ds(pl.multiple_of(k * TILE + TILE, TILE), TILE)
-        for v in range(V):
-            packed_hal[v, rows, :] = pack(lambda t: q[v, t + T * (t // 2), wide, :], 4)
-        return carry
-
-    lax.fori_loop(0, R // TILE, pack_halo, 0)
-
-    def unpack_halo(v, carry):
-        got = exact_dot(packed_hal[v], tabh[...])
-        for i in range(4):
-            around[i, v] = got[:, i * X : (i + 1) * X]
-        return carry
-
-    lax.fori_loop(0, V, unpack_halo, 0)
-
-    to_hbm = [
-        pltpu.make_async_copy(
-            q.at[:, pl.ds(T + 2, 2), pl.ds(TILE, R)], sector, out_sem.at[0]
-        )
-    ]
-    to_hbm[0].start()
+    to_hbm = []
 
     def radial(k, carry):
         rows = pl.ds(pl.multiple_of(k * TILE, TILE), TILE)
@@ -601,26 +641,43 @@
             return carry
 
         lax.fori_loop(low, high, step, 0)
-        t0, t1 = (0 if part == 0 else low - 2 - LAG), high - 2 - LAG
+        t0, t1 = (2 if part == 0 else low - 2 - LAG), high - 2 - LAG
         copy = pltpu.make_async_copy(
             out.at[:, pl.ds(t0, t1 - t0)], shared.at[:, pl.ds(t0, t1 - t0)], out_sem.at[2 + part]
         )
         copy.start()
         to_hbm.append(copy)
 
-    plane(0, False, False, True, False)
-    plane(1, False, False, True, False)
-    for s in range(2, 2 + LAG):
+    for s in range(2, 4 + LAG):
         plane(s, True, False, axial_before=s > 2)
     planes(0)
 
-    for copy in sides:
+    for copy in ends:
         copy.wait_recv()
+    for v in range(V):
+        for k in range(R // TILE):
+            before = roll(rim_in[0, v], -2 * TILE * k)
+            after = roll(rim_in[1, v], 2 * TILE - 2 * TILE * k)
+            packed_hal[v, pl.ds(k * TILE, TILE), :] = jnp.where(block_of == 0, before, after)
+
+    def unpack_halo(v, carry):
+        got = exact_dot(packed_hal[v], tabh[...])
+        for i in range(4):
+            around[i, v] = got[:, i * X : (i + 1) * X]
+        return carry
+
+    lax.fori_loop(0, V, unpack_halo, 0)
+
+    @pl.when(has_right)
+    def _():
+        sides[0].wait_recv()
+
+    @pl.when(has_left)
+    def _():
+        sides[1].wait_recv()
 
     sign = jnp.where(first, 1.0, -1.0).astype(jnp.float32)
-    has_left = (my_ax > 0).astype(jnp.int32)
-    has_right = (my_ax < n_ax - 1).astype(jnp.int32)
-    inside = jnp.where(first, has_left, has_right) == 1
+    inside = jnp.where(first, has_left.astype(jnp.int32), has_right.astype(jnp.int32)) == 1
     at = lane & (T - 1)
 
     def section(k, carry):
@@ -749,6 +806,20 @@
     start_all(send_b, recv_b, (b_send, b_recv))
     recv_b[me] = send_b[me]
     planes(2)
+    for copy in halos:
+        copy.wait_recv()
+    plane(0, False, False, True, False)
+    plane(1, False, False, True, False)
+    for s in (2, 3):
+        plane(s + LAG, False, True, False, False)
+    to_hbm.append(
+        pltpu.make_async_copy(q.at[:, pl.ds(T + 2, 2), pl.ds(TILE, R)], sector, out_sem.at[0])
+    )
+    to_hbm.append(
+        pltpu.make_async_copy(out.at[:, pl.ds(0, 2)], shared.at[:, pl.ds(0, 2)], out_sem.at[5])
+    )
+    for copy in to_hbm[-2:]:
+        copy.start()
     finish_all(send_b, recv_b, (b_send, b_recv))
 
     flag = plane_flags[block_map[my_ax]]
@@ -770,8 +841,17 @@
             res[g, v] = got[:, g * X : (g + 1) * X]
     to_hbm.append(pltpu.make_async_copy(res, edges, out_sem.at[1]))
     to_hbm[-1].start()
-    for copy in halos + sides:
+    for copy in halos + ends:
         copy.wait_send()
+
+    @pl.when(has_left)
+    def _():
+        sides[0].wait_send()
+
+    @pl.when(has_right)
+    def _():
+        sides[1].wait_send()
+
     for copy in to_hbm:
         copy.wait()
 
@@ -782,7 +862,9 @@
     smem = pl.BlockSpec(memory_space=pltpu.SMEM)
     f32, bf16 = jnp.float32, jnp.bfloat16
     tabs = spread_table(range(4))
-    tables = [jnp.asarray(x, bf16) for x in (tabs, tabs[:, : 2 * X].T, halo_table())]
+    tables = [
+        jnp.asarray(x, bf16) for x in (tabs, tabs[:, : 2 * X].T, halo_table(), pick_table())
+    ]
     dma = pltpu.SemaphoreType.DMA
     return pl.pallas_call(
         functools.partial(edges_body, n_theta, n_ax),
@@ -791,7 +873,7 @@
             jax.ShapeDtypeStruct((V, 2, R, X), f32),
             jax.ShapeDtypeStruct((V, SHARE, R, X), f32),
         ),
-        in_specs=[any_space] * 6 + [pl.BlockSpec(memory_space=pltpu.VMEM)] + [smem] * 4,
+        in_specs=[any_space] * 7 + [pl.BlockSpec(memory_space=pltpu.VMEM)] + [smem] * 4,
         out_specs=(any_space, any_space, any_space),
         scratch_shapes=[
             pltpu.VMEM((V, T + 4, PAD, X), f32),
@@ -804,8 +886,11 @@
             pltpu.VMEM((GROUPS * X, 4 * X), bf16),
             pltpu.VMEM((2 * X, GROUPS * X), bf16),
             pltpu.VMEM((X, 4 * X), bf16),
+            pltpu.VMEM((PER // 2, 4 * X, X), bf16),
             pltpu.VMEM((V + 1, R + TILE, GROUPS * X), f32),
             pltpu.VMEM((V, R, X), f32),
+            pltpu.VMEM((2, V, TILE, X), f32),
+            pltpu.VMEM((2, V, TILE, X), f32),
             pltpu.VMEM((4, V + 1, R + TILE, X), f32),
             pltpu.VMEM((4, V, R, X), f32),
             pltpu.VMEM((2, V, R, X), f32),
@@ -822,7 +907,9 @@
             pltpu.VMEM((2 * ROWS, n_theta * T), f32),
             pltpu.VMEM((GROUPS, V, R, X), f32),
             dma((GROUPS,)),
-            dma((5,)),
+            dma((6,)),
+            dma((2,)),
+            dma((2,)),
             dma((2,)),
             dma((2,)),
             dma((2,)),
@@ -831,7 +918,7 @@
             dma((n_theta,)),
             dma((n_theta,)),
             dma((n_theta,)),
-            dma((5,)),
+            dma((6,)),
         ],
         compiler_params=pltpu.CompilerParams(
             collective_id=0, has_side_effects=True, vmem_limit_bytes=60 * 1024 * 1024

time: 57.5 us -> 51.5 us (0.90)
  the two profiles are of different devices: /device:TPU:1 before, /device:TPU:25 now
where the time goes in v2:
time: 51.5 us; the launch traced here: 51.3 us
  Pallas kernels  50.6 us (98%)
  between operations  0.66 us (1%)
    pallas_call x1, Pallas kernels, edges_call(): pl.pallas_call(functools.partial(edges_body, n_theta, n_ax), out_shape=(j...  37.6 us
    pallas_call x1, Pallas kernels, section_call(): pl.pallas_call(section_body, out_shape=jax.ShapeDtypeStruct((V, T, R, X),...  13 us

profile of v2, /device:TPU:25, one launch (start us, length us, event | category | flops | bytes accessed | tf_op | source)
XLA Modules:
  0.0 51.3 jit_solution(16127094560527986200)
XLA Ops:
  0.7 37.6 %shard_map.118 = (f32[4,5,64,128]{3,2,1,0:T(8,128)}, f32[5,2,64,128]{3,2,1,0:T(8,128)}, f32[5,40,64,128]{3,2,1,0:T(8,128)}) custom-call(f32[5,64,64,128]{3,2,1,0:T(8,128)} %state.3, f32[64,64,128]{2,1,0:T(8,128)} %visc.3, f32[5,64,4,128]{3,2,1,0:T(4,128)} %rims.3, bf16[512,512]{1,0:T(8,128)(2,1)} %constant.11.clone.spread, ...), custom_call_target="tpu_custom_call" | custom-call | flops 400000000 | bytes 14000000 | tf_op jit(solution)/shard_map/pallas_call | solution.py:869
  38.3 13.0 %shard_map.119 = f32[5,64,64,128]{3,2,1,0:T(8,128)} custom-call(f32[5,64,64,128]{3,2,1,0:T(8,128)} %state.3, f32[64,64,128]{2,1,0:T(8,128)} %visc.3, f32[5,64,4,128]{3,2,1,0:T(4,128)} %rims.3, f32[5,2,64,128]{3,2,1,0:T(8,128)} %get-tuple-element.8.sector, f32[4,5,64,128]{3,2,1,0:T(8,128)} %get-tuple-element.9.edges, ...), custom_call_target="tpu_custom_call" | custom-call | flops 29491200 | bytes 24000000 | tf_op jit(solution)/shard_map/pallas_call | solution.py:327

commit v3 on v2

--- a/solution.py
+++ b/solution.py
@@ -19,7 +19,7 @@
 GROUPS = 4
 PER = 16
 CHUNK = 8
-SHARE = 40
+SHARE = 48
 LAG = 3
 ROWS = 24
 MESH = pl.DeviceIdType.MESH
@@ -399,7 +399,7 @@
     return jnp.where(n < 1024, p, -p)
 
 
-PARTS = (4 + LAG, 17, 31, SHARE + LAG + 2)
+PARTS = (4 + LAG, 21, 37, SHARE + LAG + 2)
 
 
 def edges_body(

time: 51.5 us -> 50.9 us (0.988)
  Pallas kernels: 50.6 us -> 50 us
    pallas_call x1, Pallas kernels: 13 us -> 12.3 us  [section_call(): pl.pallas_call(section_body, out_shape=jax.ShapeDtypeStruct((V, T, R, X),...]
where the time goes in v3:
time: 50.9 us; the launch traced here: 50.7 us
  Pallas kernels  50 us (98%)
  between operations  0.66 us (1%)
    pallas_call x1, Pallas kernels, edges_call(): pl.pallas_call(functools.partial(edges_body, n_theta, n_ax), out_shape=(j...  37.7 us
    pallas_call x1, Pallas kernels, section_call(): pl.pallas_call(section_body, out_shape=jax.ShapeDtypeStruct((V, T, R, X),...  12.3 us

profile of v3, /device:TPU:25, one launch (start us, length us, event | category | flops | bytes accessed | tf_op | source)
XLA Modules:
  0.0 50.7 jit_solution(4215793493422684514)
XLA Ops:
  0.7 37.7 %shard_map.118 = (f32[4,5,64,128]{3,2,1,0:T(8,128)}, f32[5,2,64,128]{3,2,1,0:T(8,128)}, f32[5,48,64,128]{3,2,1,0:T(8,128)}) custom-call(f32[5,64,64,128]{3,2,1,0:T(8,128)} %state.3, f32[64,64,128]{2,1,0:T(8,128)} %visc.3, f32[5,64,4,128]{3,2,1,0:T(4,128)} %rims.3, bf16[512,512]{1,0:T(8,128)(2,1)} %constant.11.clone.spread, ...), custom_call_target="tpu_custom_call" | custom-call | flops 400000000 | bytes 14000000 | tf_op jit(solution)/shard_map/pallas_call | solution.py:869
  38.3 12.3 %shard_map.119 = f32[5,64,64,128]{3,2,1,0:T(8,128)} custom-call(f32[5,64,64,128]{3,2,1,0:T(8,128)} %state.3, f32[64,64,128]{2,1,0:T(8,128)} %visc.3, f32[5,64,4,128]{3,2,1,0:T(4,128)} %rims.3, f32[5,2,64,128]{3,2,1,0:T(8,128)} %get-tuple-element.8.sector, f32[4,5,64,128]{3,2,1,0:T(8,128)} %get-tuple-element.9.edges, ...), custom_call_target="tpu_custom_call" | custom-call | flops 19660800 | bytes 24000000 | tf_op jit(solution)/shard_map/pallas_call | solution.py:327
